TPU v7x, 256 devices: a whole 4x4x8 slice. The times are simulated.
256 devices in a mesh: dp: 32 (over x, y, core), mp: 8 (over z).
Axes of the slice: x: 4, y: 4, z: 8, core: 2. Of those that a mesh axis runs over, the one named last changes fastest.
Arguments:
- inputs: bfloat16 [24576, 4096], P('dp'), may hold values from -6 to 6
- query_grad: bfloat16 [24576, 4096], P('dp', 'mp'), may hold values from -6 to 6
- master_weight: float32 [4096, 4096], P('dp', 'mp'), may hold values from -24 to 24
- row_factor: float32 [4096], P('dp'), may hold values from 0 to 1, as said below
- col_factor: float32 [4096], P('mp'), may hold values from 0 to 1, as said below
- step: int32 [1], replicated, may hold values from 2 to 20
Outputs:
- update: float32 [4096, 4096], P('dp', 'mp')
- new_weight: float32 [4096, 4096], P('dp', 'mp')
- row_new: float32 [4096], P('dp')
- col_new: float32 [4096], P('mp')
- next_weight: bfloat16 [4096, 4096], P(None, 'mp')
Inputs may be any that keep to these rules, and one draw needn't show every extreme that they name: `row_factor`: positive factors. `col_factor`: positive factors.
All inputs are finite; a program needn't handle non-finite values.
Results may differ from a plain program's by a relative error of at most 0.001.
Values may be sent and summed in bfloat16 or wider, within the bound.
A program may use at most 64 MiB of HBM per device.

v0:
```python
import jax
import jax.numpy as jnp
from jax import lax
from jax.sharding import PartitionSpec as P


def body(inputs, query_grad, master_weight, row_factor, col_factor, step):
    total_tokens = inputs.shape[0] * lax.axis_size("dp")
    total_rows = inputs.shape[1]
    total_cols = query_grad.shape[1] * lax.axis_size("mp")
    element_count = total_rows * total_cols
    summed = lax.psum_scatter(
        lax.dot_general(
            inputs, query_grad, (((0,), (0,)), ((), ())), preferred_element_type=jnp.float32
        ),
        "dp",
        scatter_dimension=0,
        tiled=True,
    )
    gradient = summed / total_tokens
    step_value = step[0].astype(jnp.float32)
    decay_rate = 1.0 - step_value ** (-0.8)
    squares = gradient * gradient
    weight_local = jnp.sum(master_weight * master_weight)
    row_totals = lax.psum(jnp.sum(squares, 1), "mp")
    col_totals = lax.psum(jnp.sum(squares, 0), "dp")
    row_new = decay_rate * row_factor + (1.0 - decay_rate) * (row_totals / total_cols + 1e-30)
    col_new = decay_rate * col_factor + (1.0 - decay_rate) * (col_totals / total_rows + 1e-30)
    raw_update = gradient * lax.rsqrt(row_new[:, None] * col_new[None, :])
    raw_total, weight_total = lax.psum(
        (jnp.sum(raw_update * raw_update), weight_local), ("dp", "mp")
    )
    clip_factor = jnp.maximum(1.0, jnp.sqrt(raw_total / element_count))
    update = raw_update / clip_factor
    weight_norm = jnp.sqrt(weight_total / element_count + 1e-06)
    step_size = 0.01 * weight_norm
    new_weight = master_weight - step_size * update
    next_weight = lax.all_gather(new_weight.astype(jnp.bfloat16), "dp", axis=0, tiled=True)
    return (update, new_weight, row_new, col_new, next_weight)


def solution(mesh):
    in_specs = (P("dp", None), P("dp", "mp"), P("dp", "mp"), P("dp"), P("mp"), P())
    out_specs = (P("dp", "mp"), P("dp", "mp"), P("dp"), P("mp"), P(None, "mp"))
    return jax.shard_map(body, mesh=mesh, in_specs=in_specs, out_specs=out_specs, check_vma=False)
```

profile of v0, /device:TPU:1, one launch (start us, length us, event | category | flops | bytes accessed | tf_op | source)
XLA Modules:
  0.0 338.9 jit_solution(1220448658436465562)
XLA Ops:
  7.2 0.0 copy-start
  7.2 0.0 reduce-scatter.2.cloned.1.call-start
  7.2 1.1 copy-done
  8.3 8.6 %fusion.3 = f32[4096,512]{1,0:T(8,128)} fusion(bf16[768,4096]{1,0:T(8,128)(2,1)} %param.6, bf16[768,512]{1,0:T(8,128)(2,1)S(1)} %copy-done), kind=kOutput, calls=%fused_computation.10 | convolution fusion | flops 3221225472 | bytes 15466496 | tf_op jit(solution)/shard_map/dot_general | solution.py:13
  16.9 0.0 copy-start.1
  16.9 0.0 copy-start.5
  16.9 0.0 copy-start.4
  16.9 0.0 reduce-scatter.2.cloned.1.call-update
  16.9 0.0 all-gather.2.cloned.1.call-start
  17.7 0.1 copy-done.1
  17.8 0.7 multiply_reduce_fusion
  18.5 101.0 %reduce-scatter.2.cloned.1.call-done = f32[128,512]{1,0:T(8,128)} async-done(((f32[4096,512]{1,0:T(8,128)}), f32[128,512]{1,0:T(8,128)}) %reduce-scatter.2.cloned.1.call-update) | async-done | bytes 262160 | tf_op jit(solution)/shard_map/reduce_scatter | solution.py:12
  119.5 1.1 multiply_reduce_fusion.3
  120.5 13.7 %psum.28 = f32[128]{0:T(128)S(1)} all-reduce(f32[128]{0:T(128)S(1)} %get-tuple-element.5), channel_id=1, replica_groups=mesh['dp'=32,'mp'=8] {'mp'}, use_global_device_ids=true, to_apply=%region_2.0 | all-reduce | flops 128 | bytes 1024 | tf_op jit(solution)/shard_map/psum | solution.py:25
  134.3 68.1 %psum.29 = f32[512]{0:T(512)S(1)} all-reduce(f32[512]{0:T(512)S(1)} %get-tuple-element.6), channel_id=1, replica_groups=mesh['dp'=32,'mp'=8] {'dp'}, use_global_device_ids=true, to_apply=%region_4.0 | all-reduce | flops 512 | bytes 4096 | tf_op jit(solution)/shard_map/psum | solution.py:26
  202.3 0.0 copy-done.5
  202.4 0.0 copy-done.4
  202.4 0.0 copy-start.3
  202.4 0.0 copy-start.2
  202.4 1.7 multiply_reduce_fusion.1
  204.1 72.7 %all-reduce = (f32[]{:T(128)}, f32[]{:T(128)}) all-reduce(f32[]{:T(128)} %multiply_reduce_fusion.1, f32[]{:T(128)} %multiply_reduce_fusion), channel_id=1, replica_groups=mesh['dp'=32,'mp'=8] {'dp','mp'}, use_global_device_ids=true, to_apply=%region_6.0 | all-reduce | flops 2 | bytes 16 | tf_op jit(solution)/shard_map/psum | solution.py:30
  278.1 1.9 fusion.1
  280.1 0.0 all-gather.2.cloned.1.call-update
  280.1 47.5 %all-gather.2.cloned.1.call-done = bf16[4096,512]{1,0:T(8,128)(2,1)} async-done(((bf16[128,512]{1,0:T(8,128)(2,1)}), bf16[4096,512]{1,0:T(8,128)(2,1)}) %all-gather.2.cloned.1.call-update) | async-done | bytes 4194320 | tf_op jit(solution)/shard_map/all_gather | solution.py:38
  327.6 4.5 %copy.13 = bf16[4096,512]{1,0:T(8,128)(2,1)} copy(bf16[4096,512]{1,0:T(8,128)(2,1)} %all-gather.2.cloned.1.call-done) | data formatting | bytes 8388608
  332.0 0.0 copy-done.3
  332.0 0.0 copy-done.2
  (2 shorter events, 0.0 us)
Async XLA Ops:
  7.2 1.1 copy-start
  7.2 112.3 %reduce-scatter.2.cloned.1.call-start = ((), (), s32[]{:S(2)}) async-start(), calls=%async_computation.1 | async-start | bytes 8650752 | tf_op jit(solution)/shard_map/reduce_scatter | solution.py:12
  16.9 0.9 copy-start.1
  16.9 185.5 %copy-start.5 = (f32[128]{0:T(128)S(1)}, f32[128]{0:T(128)}, u32[]{:S(2)}) copy-start(f32[128]{0:T(128)} %param.9) | copy-start | bytes 1540
  16.9 185.5 %copy-start.4 = (f32[512]{0:T(512)S(1)}, f32[512]{0:T(512)}, u32[]{:S(2)}) copy-start(f32[512]{0:T(512)} %param.10) | copy-start | bytes 6148
  16.9 310.7 %all-gather.2.cloned.1.call-start = ((), (), s32[]{:S(2)}) async-start(), calls=%async_computation.2 | async-start | bytes 4325376 | tf_op jit(solution)/shard_map/all_gather | solution.py:38
  202.4 129.7 %copy-start.3 = (f32[128]{0:T(128)}, f32[128]{0:T(128)S(1)}, u32[]{:S(2)}) copy-start(f32[128]{0:T(128)S(1)} %multiply_add_fusion.1) | copy-start | bytes 1540
  202.4 129.6 %copy-start.2 = (f32[512]{0:T(512)}, f32[512]{0:T(512)S(1)}, u32[]{:S(2)}) copy-start(f32[512]{0:T(512)S(1)} %multiply_add_fusion) | copy-start | bytes 6148
Sparse Core Ops, SparseCore 0:
  17.0 102.4 reduce-scatter.1
  280.2 47.3 all-gather.1
where the time goes:
time: 339 us
  blocking collectives  154 us (45%)
  waiting for transfers between devices  148 us (44%)
  between operations  16.2 us (5%)
  matrix products  8.57 us (3%)
  local copies, waits for them, and re-layouts  5.71 us (2%)
  other arithmetic  5.36 us (2%)
    reduce_scatter x1, waiting for transfers between devices, body(): lax.psum_scatter(lax.dot_general(inputs, query_grad, (((0,), (0,)), ((),...  101 us
    psum x1, blocking collectives, body(): lax.psum((jnp.sum(raw_update * raw_update), weight_local), ('dp', 'mp'))  72.7 us
    psum x1, blocking collectives, body(): col_totals = lax.psum(jnp.sum(squares, 0), 'dp')  68.1 us
    all_gather x1, waiting for transfers between devices, body(): lax.all_gather(new_weight.astype(jnp.bfloat16), 'dp', axis=0, tiled=True)  47.5 us
    psum x1, blocking collectives, body(): row_totals = lax.psum(jnp.sum(squares, 1), 'mp')  13.7 us
    dot_general x1, matrix products, body(): lax.dot_general(inputs, query_grad, (((0,), (0,)), ((), ())), preferred_e...  8.57 us
  transfers between devices with their start and end apart: 2, of which 2 were waited for; matrix products, arithmetic and copies ran while one was open for 0% of the time, Pallas kernels for 0%

commit v1 on v0

v1 whole, which is shorter than its diff:
```python
import functools

import jax
import jax.numpy as jnp
from jax import lax
from jax.experimental import pallas as pl
from jax.experimental.pallas import tpu as pltpu
from jax.sharding import PartitionSpec as P

MESH = pl.DeviceIdType.MESH
NX, NY, NC = 4, 4, 2
NPLANE = NX * NY * NC
FAR = (2, 1, 3, 0)
PEAK = 32766.0
TOP = PEAK * PEAK * (1.0 - 1e-4)


def encode(x, buf):
    h = x.shape[0]
    top = jnp.max(jnp.abs(x), axis=0, keepdims=True)
    e = jnp.ceil(jnp.log2(jnp.maximum(top, 1e-30)))
    t = x * (jnp.exp2(-e) * TOP)
    y = t * lax.rsqrt(jnp.maximum(jnp.abs(t), 1e-12))
    buf[0:h, :] = jnp.round(y).astype(jnp.int32).astype(jnp.int16)
    buf[h : h + 16, :] = jnp.broadcast_to(e.astype(jnp.int32), (16, x.shape[1])).astype(jnp.int16)


def decode(buf, h):
    y = buf[0:h, :].astype(jnp.int32).astype(jnp.float32)
    e = buf[h : h + 16, :].astype(jnp.int32).astype(jnp.float32)[0:1, :]
    return y * jnp.abs(y) * (jnp.exp2(e) * (1.0 / TOP))


def kernel(
    nz, total_tokens, total_rows, total_cols,
    x_hbm, q_hbm, mw_ref, row_ref, col_ref, step_ref,
    upd_ref, nw_ref, rown_ref, coln_ref, out_ref,
    qcat, qT, X, S, R,
    s1a, r1a, s1b, r1b, s2a, r2a, s2b, r2b,
    zr, pr, ta, tb,
    own_sem, qsem, d_send, d_recv,
    s1a_s, s1a_r, s1b_s, s1b_r, s2a_s, s2a_r, s2b_s, s2b_r,
    ex_s, zr_r, pr_r, ta_r, tb_r, zs1, zs2,
    ag_s, a1_r, a2_r, b1_r, b2_r, dd_r, dd2_r,
):
    T, W = q_hbm.shape
    B = W // 1
    H = W // 2
    dp = lax.axis_index("dp")
    z = lax.axis_index("mp")
    c = dp % 2
    cx = dp // (NY * NC)
    cy = (dp // NC) % NY
    sib = dp + 1 - 2 * c
    cs = 1 - c
    u = cx * (1 - c) + cy * c
    w = cy * (1 - c) + cx * c
    su = NY * NC - (NY * NC - NC) * c
    sw = NC + (NY * NC - NC) * c
    us, ws, sus, sws = w, u, sw, su

    def dev(uu, ww):
        return ((uu + 8) % 4) * su + ((ww + 8) % 4) * sw + c

    def sdev(uu, ww):
        return ((uu + 8) % 4) * sus + ((ww + 8) % 4) * sws + cs

    un, up = dev(u + 1, w), dev(u - 1, w)
    wn, wp = dev(u, w + 1), dev(u, w - 1)

    def cols_of(b):
        return pl.ds(pl.multiple_of(b * 128, 128), 128)

    def remote(src, dst, ss, rs, d, zz=None):
        return pltpu.make_async_remote_copy(
            src, dst, ss, rs, device_id=(d, z if zz is None else zz), device_id_type=MESH
        )

    pltpu.make_async_copy(q_hbm, qcat.at[pl.ds(0, T)], qsem).start()
    own = []
    for g in range(4):
        for k in range(4):
            s = 4 * g + k
            cp = pltpu.make_async_copy(
                x_hbm.at[:, cols_of(dev(u + FAR[g], w + FAR[k]))],
                X.at[s // 2, pl.ds(0, T), pl.ds(128 * (s % 2), 128)],
                own_sem.at[s],
            )
            cp.start()
            own.append(cp)

    bar = pltpu.get_barrier_semaphore()
    zn, zp = (z + 1) % nz, (z + nz - 1) % nz
    for d in (sib, un, up, wn, wp):
        pl.semaphore_signal(bar, 1, device_id=(d, z), device_id_type=MESH)
    for zz in (zn, zp):
        pl.semaphore_signal(bar, 1, device_id=(dp, zz), device_id_type=MESH)
    pl.semaphore_wait(bar, 7)

    dq = remote(q_hbm, qcat.at[pl.ds(T, T)], d_send.at[16], d_recv.at[16], sib)
    dq.start()
    dx = []
    for g in range(4):
        for k in range(4):
            s = 4 * g + k
            cp = remote(
                x_hbm.at[:, cols_of(sdev(us + FAR[g], ws + FAR[k]))],
                X.at[s // 2, pl.ds(T, T), pl.ds(128 * (s % 2), 128)],
                d_send.at[s], d_recv.at[s], sib,
            )
            cp.start()
            dx.append(cp)
    for zz in (zn, zp):
        pl.semaphore_signal(zs1, 1, device_id=(dp, zz), device_id_type=MESH)

    pltpu.make_async_copy(q_hbm, qcat.at[pl.ds(0, T)], qsem).wait()
    qT[:, 0:T] = qcat[0:T, :].T
    dq.wait_recv()
    qT[:, T : 2 * T] = qcat[T : 2 * T, :].T

    def matmul(p):
        for s in (2 * p, 2 * p + 1):
            own[s].wait()
            dx[s].wait_recv()
        acc = jnp.dot(qT[...], X[p], preferred_element_type=jnp.float32)
        S[2 * p] = acc[:, 0:128]
        S[2 * p + 1] = acc[:, 128:256]

    c1a = {}
    for p in range(2):
        matmul(p)
        for k in (2 * p, 2 * p + 1):
            for d, to in ((0, un), (1, up)):
                encode(S[k, d * H : d * H + H, :], s1a.at[d, k])
                cp = remote(s1a.at[d, k], r1a.at[d, k], s1a_s.at[d, k], s1a_r.at[d, k], to)
                cp.start()
                c1a[d, k] = cp
    pl.semaphore_wait(zs1, 2)
    for zz in ((z + 2) % nz, (z + nz - 2) % nz):
        pl.semaphore_signal(zs2, 1, device_id=(dp, zz), device_id_type=MESH)
    for p in range(2, 8):
        matmul(p)

    c1b = {}

    def send1b(d, k, h):
        to = un if d == 0 else up
        cp = remote(
            s1b.at[d, k, h], r1b.at[d, k, h], s1b_s.at[d, k, h], s1b_r.at[d, k, h], to
        )
        cp.start()
        c1b[d, k, h] = cp

    for k in range(4):
        for d in range(2):
            g = 1 + d
            h = 1 - d
            encode(S[4 * g + k, h * H : h * H + H, :], s1b.at[d, k, h])
            send1b(d, k, h)
        for d in range(2):
            g = 1 + d
            h = d
            c1a[d, k].wait_recv()
            encode(S[4 * g + k, h * H : h * H + H, :] + decode(r1a.at[d, k], H), s1b.at[d, k, h])
            send1b(d, k, h)

    pl.semaphore_wait(zs2, 2)

    c2a, c2b = {}, {}

    def send2b(d, h):
        to = wn if d == 0 else wp
        cp = remote(s2b.at[d, h], r2b.at[d, h], s2b_s.at[d, h], s2b_r.at[d, h], to)
        cp.start()
        c2b[d, h] = cp

    for k in range(4):
        for h in range(2):
            c1b[0, k, h].wait_recv()
            c1b[1, k, h].wait_recv()
            R[k, h * H : h * H + H, :] = (
                S[12 + k, h * H : h * H + H, :]
                + decode(r1b.at[0, k, h], H)
                + decode(r1b.at[1, k, h], H)
            )
        if k == 0:
            for d, to in ((0, wn), (1, wp)):
                encode(R[0, d * H : d * H + H, :], s2a.at[d])
                cp = remote(s2a.at[d], r2a.at[d], s2a_s.at[d], s2a_r.at[d], to)
                cp.start()
                c2a[d] = cp
        elif k < 3:
            d = k - 1
            h = 1 - d
            encode(R[k, h * H : h * H + H, :], s2b.at[d, h])
            send2b(d, h)
            c2a[d].wait_recv()
            h = d
            encode(R[k, h * H : h * H + H, :] + decode(r2a.at[d], H), s2b.at[d, h])
            send2b(d, h)
    for h in range(2):
        c2b[0, h].wait_recv()
        c2b[1, h].wait_recv()
        R[3, h * H : h * H + H, :] = (
            R[3, h * H : h * H + H, :] + decode(r2b.at[0, h], H) + decode(r2b.at[1, h], H)
        )

    gT = R[3] * (1.0 / total_tokens)
    zr[pl.ds(z, 1)] = jnp.sum(gT * gT, axis=0, keepdims=True)[None]
    gN = gT.T
    pr[pl.ds(dp, 1)] = jnp.sum(gN * gN, axis=0, keepdims=True)[None]

    def to_plane(i, buf, ssem, rsem):
        peer = (dp + i) % NPLANE
        return remote(buf.at[pl.ds(dp, 1)], buf.at[pl.ds(dp, 1)], ssem, rsem, peer)

    def to_z(i, buf, ssem, rsem):
        peer = (z + i) % nz
        return remote(buf.at[pl.ds(z, 1)], buf.at[pl.ds(z, 1)], ssem, rsem, dp, peer)

    def exchange(n, to, buf, ssem, rsem):
        def body(i, carry):
            to(i, buf, ssem, rsem).start()
            return carry

        lax.fori_loop(1, n, body, 0)

    def finish(n, buf, rsem):
        part = buf.at[pl.ds(0, n - 1)]
        cp = pltpu.make_async_copy(part, part, rsem)
        cp.wait()

    exchange(nz, to_z, zr, ex_s.at[0], zr_r)
    exchange(NPLANE, to_plane, pr, ex_s.at[1], pr_r)
    mw = mw_ref[...]
    wsum = jnp.sum(mw * mw)
    stepv = jnp.full((1, 128), step_ref[0].astype(jnp.float32), jnp.float32)
    decay = 1.0 - jnp.exp(-0.8 * jnp.log(stepv))
    decay_w = jnp.concatenate([decay] * (W // 128), axis=1)
    finish(nz, zr, zr_r)
    row_new = decay * row_ref[...] + (1.0 - decay) * (jnp.sum(zr[...], axis=0) / total_cols + 1e-30)
    rown_ref[...] = row_new
    half = (gT * lax.rsqrt(row_new)).T
    finish(NPLANE, pr, pr_r)
    col_new = decay_w * col_ref[...] + (1.0 - decay_w) * (
        jnp.sum(pr[...], axis=0) / total_rows + 1e-30
    )
    coln_ref[...] = col_new
    raw = half * lax.rsqrt(col_new)
    rsum = jnp.sum(raw * raw)

    lane = lax.broadcasted_iota(jnp.int32, (1, 1, 128), 2)
    ta[pl.ds(dp, 1)] = jnp.where(lane < 64, rsum, wsum)
    exchange(NPLANE, to_plane, ta, ex_s.at[2], ta_r)
    finish(NPLANE, ta, ta_r)
    tb[pl.ds(z, 1)] = jnp.sum(ta[...], axis=0, keepdims=True)
    exchange(nz, to_z, tb, ex_s.at[3], tb_r)
    finish(nz, tb, tb_r)
    tot = jnp.sum(tb[...], axis=0) / (total_rows * total_cols)
    clip = jnp.maximum(1.0, jnp.sqrt(tot[:, 0:1]))
    size = 0.01 * jnp.sqrt(tot[:, 64:65] + 1e-06)
    upd = raw * (1.0 / clip)
    nw = mw - size * upd

    def rows_of(b, half=None):
        if half is None:
            return out_ref.at[pl.ds(pl.multiple_of(b * 128, 128), 128)]
        return out_ref.at[pl.ds(pl.multiple_of(b * 128 + half * 64, 64), 64)]

    mine = rows_of(dp)
    mine[...] = nw.astype(jnp.bfloat16)

    sent = []

    def push(b, half, sem, rsem, to):
        cp = remote(rows_of(b, half), rows_of(b, half), sem, rsem, to)
        cp.start()
        sent.append(cp)
        return cp

    n_sent = [0]

    def nsem():
        n_sent[0] += 1
        return ag_s.at[n_sent[0] - 1]

    a1 = {0: push(dp, None, nsem(), a1_r.at[0], wn), 1: push(dp, None, nsem(), a1_r.at[1], wp)}
    b1, b2, dd, dd2, a2 = {}, {}, {}, {}, {}

    def spread(b, k):
        b1[0, k] = push(b, None, nsem(), b1_r.at[0, k], un)
        b1[1, k] = push(b, None, nsem(), b1_r.at[1, k], up)

    def across(b, j):
        dd[j] = push(b, None, nsem(), dd_r.at[j], sib)

    spread(dp, 0)
    across(dp, 0)
    upd_ref[...] = upd
    nw_ref[...] = nw
    a1[0].wait_recv()
    a2[0] = push(wp, 0, nsem(), a2_r.at[0], wn)
    spread(wp, 1)
    a1[1].wait_recv()
    a2[1] = push(wn, 1, nsem(), a2_r.at[1], wp)
    spread(wn, 2)
    across(wp, 1)
    across(wn, 2)

    def onward(k, ww):
        b1[0, k].wait_recv()
        b2[0, k] = push(dev(u - 1, ww), 0, nsem(), b2_r.at[0, k], un)
        across(dev(u - 1, ww), 4 + 2 * k)
        b1[1, k].wait_recv()
        b2[1, k] = push(dev(u + 1, ww), 1, nsem(), b2_r.at[1, k], up)
        across(dev(u + 1, ww), 5 + 2 * k)

    onward(0, w)
    a2[0].wait_recv()
    a2[1].wait_recv()
    wf = dev(u, w + 2)
    spread(wf, 3)
    across(wf, 3)
    onward(1, w - 1)
    onward(2, w + 1)
    onward(3, w + 2)
    for k, ww in ((0, w), (1, w - 1), (2, w + 1), (3, w + 2)):
        b2[0, k].wait_recv()
        b2[1, k].wait_recv()
        dd2[k] = push(dev(u + 2, ww), None, nsem(), dd2_r.at[k], sib)
    for j in range(12):
        dd[j].wait_recv()
    for k in range(4):
        dd2[k].wait_recv()

    for cp in sent:
        cp.wait_send()
    dq.wait_send()
    for cp in dx:
        cp.wait_send()
    for group in (c1a, c1b, c2a, c2b):
        for cp in group.values():
            cp.wait_send()
    for i, (buf, n) in enumerate(((zr, nz), (pr, NPLANE), (ta, NPLANE), (tb, nz))):
        finish(n, buf, ex_s.at[i])


def body(inputs, query_grad, master_weight, row_factor, col_factor, step):
    T, W = query_grad.shape
    rows = inputs.shape[1]
    nz = lax.axis_size("mp")
    ndp = lax.axis_size("dp")
    H = W // 2
    f32, i16, bf16 = jnp.float32, jnp.int16, jnp.bfloat16
    DMA = pltpu.SemaphoreType.DMA
    hb = (H + 16, 128)
    vm = pl.BlockSpec(memory_space=pltpu.VMEM)
    hbm = pl.BlockSpec(memory_space=pl.ANY)
    outs = pl.pallas_call(
        functools.partial(kernel, nz, T * ndp, rows, W * nz),
        out_shape=[
            jax.ShapeDtypeStruct((128, W), f32),
            jax.ShapeDtypeStruct((128, W), f32),
            jax.ShapeDtypeStruct((1, 128), f32),
            jax.ShapeDtypeStruct((1, W), f32),
            pltpu.VMEM((rows, W), bf16),
        ],
        in_specs=[hbm, hbm, vm, vm, vm, pl.BlockSpec(memory_space=pltpu.SMEM)],
        out_specs=[vm, vm, vm, vm, vm],
        scratch_shapes=[
            pltpu.VMEM((2 * T, W), bf16),
            pltpu.VMEM((W, 2 * T), bf16),
            pltpu.VMEM((8, 2 * T, 256), bf16),
            pltpu.VMEM((16, W, 128), f32),
            pltpu.VMEM((4, W, 128), f32),
            pltpu.VMEM((2, 4) + hb, i16),
            pltpu.VMEM((2, 4) + hb, i16),
            pltpu.VMEM((2, 4, 2) + hb, i16),
            pltpu.VMEM((2, 4, 2) + hb, i16),
            pltpu.VMEM((2,) + hb, i16),
            pltpu.VMEM((2,) + hb, i16),
            pltpu.VMEM((2, 2) + hb, i16),
            pltpu.VMEM((2, 2) + hb, i16),
            pltpu.VMEM((nz, 1, 128), f32),
            pltpu.VMEM((NPLANE, 1, W), f32),
            pltpu.VMEM((NPLANE, 1, 128), f32),
            pltpu.VMEM((nz, 1, 128), f32),
            DMA((16,)), DMA, DMA((17,)), DMA((17,)),
            DMA((2, 4)), DMA((2, 4)), DMA((2, 4, 2)), DMA((2, 4, 2)),
            DMA((2,)), DMA((2,)), DMA((2, 2)), DMA((2, 2)),
            DMA((4,)), DMA, DMA, DMA, DMA,
            pltpu.SemaphoreType.REGULAR, pltpu.SemaphoreType.REGULAR,
            DMA((40,)), DMA((2,)), DMA((2,)), DMA((2, 4)), DMA((2, 4)), DMA((12,)), DMA((4,)),
        ],
        compiler_params=pltpu.CompilerParams(
            collective_id=0, has_side_effects=True, vmem_limit_bytes=44 * 2**20
        ),
    )(
        inputs, query_grad, master_weight,
        row_factor.reshape(1, 128), col_factor.reshape(1, W), step,
    )
    return outs[0], outs[1], outs[2].reshape(128), outs[3].reshape(W), outs[4]


def solution(mesh):
    in_specs = (P("dp", None), P("dp", "mp"), P("dp", "mp"), P("dp"), P("mp"), P())
    out_specs = (P("dp", "mp"), P("dp", "mp"), P("dp"), P("mp"), P(None, "mp"))
    return jax.shard_map(body, mesh=mesh, in_specs=in_specs, out_specs=out_specs, check_vma=False)
```

time: 339 us -> 77.4 us (0.23)
  blocking collectives: 154 us -> 0 us
  waiting for transfers between devices: 148 us -> 0 us
  Pallas kernels: 0 us -> 68 us
  between operations: 16.2 us -> 1.3 us
  matrix products: 8.57 us -> 0 us
  other arithmetic: 5.36 us -> 0 us
    psum x3 -> x0, blocking collectives: 154 us -> none  [the longest x1 72.7 us: body(): lax.psum((jnp.sum(raw_update * raw_update), weight_local), ('dp', 'mp'))]
    reduce_scatter x1 -> x0, waiting for transfers between devices: 101 us -> none  [body(): lax.psum_scatter(lax.dot_general(inputs, query_grad, (((0,), (0,)), ((),...]
    pallas_call x0 -> x1, Pallas kernels: none -> 68 us  [body(): pl.pallas_call(functools.partial(kernel, nz, T * ndp, rows, W * nz), out_...]
    all_gather x1 -> x0, waiting for transfers between devices: 47.5 us -> none  [body(): lax.all_gather(new_weight.astype(jnp.bfloat16), 'dp', axis=0, tiled=True)]
    dot_general x1 -> x0, matrix products: 8.57 us -> none  [body(): lax.dot_general(inputs, query_grad, (((0,), (0,)), ((), ())), preferred_e...]
    reduce_sum x3 -> x0, other arithmetic: 3.43 us -> none  [the longest x1 1.7 us: body(): jnp.sum(raw_update * raw_update)]
  transfers between devices with their start and end apart: 2 -> 0, of which waited for: 2 -> 0; matrix products, arithmetic and copies ran while one was open for 0% -> 0% of each run, Pallas kernels for 0% -> 0%
where the time goes in v1:
time: 77.4 us; the launch traced here: 77.2 us
  Pallas kernels  68 us (88%)
  local copies, waits for them, and re-layouts  7.92 us (10%)
  between operations  1.3 us (2%)
    pallas_call x1, Pallas kernels, body(): pl.pallas_call(functools.partial(kernel, nz, T * ndp, rows, W * nz), out_...  68 us
    unnamed x13, local copies, waits for them, and re-layouts  7.92 us

profile of v1, /device:TPU:1, one launch (start us, length us, event | category | flops | bytes accessed | tf_op | source)
XLA Modules:
  0.0 77.2 jit_solution(16348511898406711761)
XLA Ops:
  1.3 0.0 copy-start
  1.3 1.1 %copy-done = bf16[768,512]{1,0:T(8,128)(2,1)S(1)} copy-done((bf16[768,512]{1,0:T(8,128)(2,1)S(1)}, bf16[768,512]{1,0:T(8,128)(2,1)}, u32[]{:S(2)}) %copy-start) | copy-done | bytes 786456
  2.4 0.0 copy-start.1
  2.4 0.9 %copy-done.1 = f32[128,512]{1,0:T(8,128)S(1)} copy-done((f32[128,512]{1,0:T(8,128)S(1)}, f32[128,512]{1,0:T(8,128)}, u32[]{:S(2)}) %copy-start.1) | copy-done | bytes 262168
  3.4 0.0 copy-start.2
  3.4 0.7 copy-done.2
  4.0 0.0 copy-start.3
  4.0 0.7 copy-done.3
  4.7 68.0 %shard_map.101 = (f32[128,512]{1,0:T(8,128)S(1)}, f32[128,512]{1,0:T(8,128)S(1)}, f32[1,128]{1,0:T(1,128)S(1)}, f32[1,512]{1,0:T(1,128)S(1)}, bf16[4096,512]{1,0:T(8,128)(2,1)S(1)}) custom-call(bf16[768,4096]{1,0:T(8,128)(2,1)} %x_hbm.1, bf16[768,512]{1,0:T(8,128)(2,1)S(1)} %copy-done, f32[128,512]{1,0:T(8,128)S(1)} %copy-done.1, f32[1,128]{1,0:T(1,128)S(1)} %bitcast.6, ...), custom_call_target="tpu_custom_call" | custom-call | tf_op jit(solution)/shard_map/pallas_call | solution.py:359
  72.7 2.0 %copy.16 = bf16[4096,512]{1,0:T(8,128)(2,1)} copy(bf16[4096,512]{1,0:T(8,128)(2,1)S(1)} %get-tuple-element.19) | data formatting | bytes 8388608
  74.7 0.7 copy.18
  75.4 0.7 copy.19
  76.1 0.5 copy.20
  76.6 0.6 copy.21
Async XLA Ops:
  1.3 1.1 %copy-start = (bf16[768,512]{1,0:T(8,128)(2,1)S(1)}, bf16[768,512]{1,0:T(8,128)(2,1)}, u32[]{:S(2)}) copy-start(bf16[768,512]{1,0:T(8,128)(2,1)} %q_hbm.1) | copy-start | bytes 2359300
  2.4 0.9 %copy-start.1 = (f32[128,512]{1,0:T(8,128)S(1)}, f32[128,512]{1,0:T(8,128)}, u32[]{:S(2)}) copy-start(f32[128,512]{1,0:T(8,128)} %mw_ref.1) | copy-start | bytes 786436
  3.4 0.7 copy-start.2
  4.0 0.7 copy-start.3

commit v2 on v1

--- a/solution.py
+++ b/solution.py
@@ -33,18 +33,18 @@
 
 def kernel(
     nz, total_tokens, total_rows, total_cols,
-    x_hbm, q_hbm, mw_ref, row_ref, col_ref, step_ref,
+    x_hbm, q_hbm, mw_hbm, row_hbm, col_hbm, step_ref,
     upd_ref, nw_ref, rown_ref, coln_ref, out_ref,
-    qcat, qT, X, S, R,
+    mw_ref, row_ref, col_ref, p_sem,
+    qcat, qT, X, S, R, sd, rd,
     s1a, r1a, s1b, r1b, s2a, r2a, s2b, r2b,
     zr, pr, ta, tb,
     own_sem, qsem, d_send, d_recv,
     s1a_s, s1a_r, s1b_s, s1b_r, s2a_s, s2a_r, s2b_s, s2b_r,
     ex_s, zr_r, pr_r, ta_r, tb_r, zs1, zs2,
-    ag_s, a1_r, a2_r, b1_r, b2_r, dd_r, dd2_r,
+    ag_s, a1_r, a2_r, b1_r, b2_r, dd_r,
 ):
     T, W = q_hbm.shape
-    B = W // 1
     H = W // 2
     dp = lax.axis_index("dp")
     z = lax.axis_index("mp")
@@ -76,18 +76,25 @@
             src, dst, ss, rs, device_id=(d, z if zz is None else zz), device_id_type=MESH
         )
 
-    pltpu.make_async_copy(q_hbm, qcat.at[pl.ds(0, T)], qsem).start()
-    own = []
-    for g in range(4):
-        for k in range(4):
-            s = 4 * g + k
+    cq = pltpu.make_async_copy(q_hbm, qcat, qsem)
+    cq.start()
+    loads = {}
+
+    def load(side, p):
+        for s in (2 * p, 2 * p + 1):
+            o = (FAR[s // 4], FAR[s % 4])
+            b = dev(u + o[0], w + o[1]) if side else sdev(us + o[0], ws + o[1])
+            j = 16 * side + s
             cp = pltpu.make_async_copy(
-                x_hbm.at[:, cols_of(dev(u + FAR[g], w + FAR[k]))],
-                X.at[s // 2, pl.ds(0, T), pl.ds(128 * (s % 2), 128)],
-                own_sem.at[s],
+                x_hbm.at[:, cols_of(b)],
+                X.at[j // 2, :, pl.ds(128 * (j % 2), 128)],
+                own_sem.at[j],
             )
             cp.start()
-            own.append(cp)
+            loads[j] = cp
+
+    for side, p in ((0, 0), (0, 1)):
+        load(side, p)
 
     bar = pltpu.get_barrier_semaphore()
     zn, zp = (z + 1) % nz, (z + nz - 1) % nz
@@ -95,51 +102,75 @@
         pl.semaphore_signal(bar, 1, device_id=(d, z), device_id_type=MESH)
     for zz in (zn, zp):
         pl.semaphore_signal(bar, 1, device_id=(dp, zz), device_id_type=MESH)
+
+    for side, p in (
+        (1, 0), (1, 1), (0, 2), (0, 4), (0, 3), (0, 5),
+        (1, 2), (1, 4), (1, 3), (1, 5), (0, 6), (0, 7), (1, 6), (1, 7),
+    ):
+        load(side, p)
+    cq.wait()
+    qT[...] = qcat[...].T
+
+    def matmul(side, p):
+        j = 8 * side + p
+        loads[2 * j].wait()
+        loads[2 * j + 1].wait()
+        return jnp.dot(qT[...], X[j], preferred_element_type=jnp.float32)
+
+    def theirs(p):
+        acc = matmul(0, p)
+        for i in range(2):
+            for h in range(2):
+                encode(acc[h * H : h * H + H, 128 * i : 128 * i + 128], sd.at[2 * p + i, h])
+
+    cd = {}
+
+    def give(p):
+        for s in (2 * p, 2 * p + 1):
+            cd[s] = remote(sd.at[s], rd.at[s], d_send.at[s], d_recv.at[s], sib)
+            cd[s].start()
+
+    def mine(p):
+        acc = matmul(1, p)
+        S[2 * p] = acc[:, 0:128]
+        S[2 * p + 1] = acc[:, 128:256]
+
+    def total(s):
+        cd[s].wait_recv()
+        for h in range(2):
+            S[s, h * H : h * H + H, :] = S[s, h * H : h * H + H, :] + decode(rd.at[s, h], H)
+
+    theirs(0)
     pl.semaphore_wait(bar, 7)
-
-    dq = remote(q_hbm, qcat.at[pl.ds(T, T)], d_send.at[16], d_recv.at[16], sib)
-    dq.start()
-    dx = []
-    for g in range(4):
-        for k in range(4):
-            s = 4 * g + k
-            cp = remote(
-                x_hbm.at[:, cols_of(sdev(us + FAR[g], ws + FAR[k]))],
-                X.at[s // 2, pl.ds(T, T), pl.ds(128 * (s % 2), 128)],
-                d_send.at[s], d_recv.at[s], sib,
-            )
-            cp.start()
-            dx.append(cp)
+    give(0)
+    theirs(1)
+    give(1)
+    params = [
+        pltpu.make_async_copy(a, b, p_sem.at[i])
+        for i, (a, b) in enumerate(((mw_hbm, mw_ref), (row_hbm, row_ref), (col_hbm, col_ref)))
+    ]
+    for cp in params:
+        cp.start()
+
     for zz in (zn, zp):
         pl.semaphore_signal(zs1, 1, device_id=(dp, zz), device_id_type=MESH)
-
-    pltpu.make_async_copy(q_hbm, qcat.at[pl.ds(0, T)], qsem).wait()
-    qT[:, 0:T] = qcat[0:T, :].T
-    dq.wait_recv()
-    qT[:, T : 2 * T] = qcat[T : 2 * T, :].T
-
-    def matmul(p):
-        for s in (2 * p, 2 * p + 1):
-            own[s].wait()
-            dx[s].wait_recv()
-        acc = jnp.dot(qT[...], X[p], preferred_element_type=jnp.float32)
-        S[2 * p] = acc[:, 0:128]
-        S[2 * p + 1] = acc[:, 128:256]
+    mine(0)
+    mine(1)
+    theirs(2)
+    give(2)
 
     c1a = {}
-    for p in range(2):
-        matmul(p)
-        for k in (2 * p, 2 * p + 1):
-            for d, to in ((0, un), (1, up)):
-                encode(S[k, d * H : d * H + H, :], s1a.at[d, k])
-                cp = remote(s1a.at[d, k], r1a.at[d, k], s1a_s.at[d, k], s1a_r.at[d, k], to)
-                cp.start()
-                c1a[d, k] = cp
+    for k in range(4):
+        total(k)
+        for d in range(2):
+            encode(S[k, d * H : d * H + H, :], s1a.at[d, k])
+        for d, to in ((0, un), (1, up)):
+            cp = remote(s1a.at[d, k], r1a.at[d, k], s1a_s.at[d, k], s1a_r.at[d, k], to)
+            cp.start()
+            c1a[d, k] = cp
     pl.semaphore_wait(zs1, 2)
     for zz in ((z + 2) % nz, (z + nz - 2) % nz):
         pl.semaphore_signal(zs2, 1, device_id=(dp, zz), device_id_type=MESH)
-    for p in range(2, 8):
-        matmul(p)
 
     c1b = {}
 
@@ -151,18 +182,50 @@
         cp.start()
         c1b[d, k, h] = cp
 
-    for k in range(4):
+    def at_once(k):
         for d in range(2):
-            g = 1 + d
             h = 1 - d
-            encode(S[4 * g + k, h * H : h * H + H, :], s1b.at[d, k, h])
-            send1b(d, k, h)
+            total(4 * (1 + d) + k)
+            encode(S[4 * (1 + d) + k, h * H : h * H + H, :], s1b.at[d, k, h])
         for d in range(2):
-            g = 1 + d
+            send1b(d, k, 1 - d)
+
+    def with_far(k):
+        for d in range(2):
             h = d
             c1a[d, k].wait_recv()
-            encode(S[4 * g + k, h * H : h * H + H, :] + decode(r1a.at[d, k], H), s1b.at[d, k, h])
-            send1b(d, k, h)
+            encode(
+                S[4 * (1 + d) + k, h * H : h * H + H, :] + decode(r1a.at[d, k], H),
+                s1b.at[d, k, h],
+            )
+        for d in range(2):
+            send1b(d, k, d)
+
+    theirs(4)
+    give(4)
+    mine(2)
+    mine(4)
+    at_once(0)
+    at_once(1)
+    for p in (3, 5):
+        theirs(p)
+        give(p)
+    mine(3)
+    mine(5)
+    with_far(0)
+    at_once(2)
+    with_far(1)
+    theirs(6)
+    give(6)
+    at_once(3)
+    with_far(2)
+    theirs(7)
+    give(7)
+    mine(6)
+    with_far(3)
+    mine(7)
+    for s in range(12, 16):
+        total(s)
 
     pl.semaphore_wait(zs2, 2)
 
@@ -205,6 +268,8 @@
             R[3, h * H : h * H + H, :] + decode(r2b.at[0, h], H) + decode(r2b.at[1, h], H)
         )
 
+    for cp in params:
+        cp.wait()
     gT = R[3] * (1.0 / total_tokens)
     zr[pl.ds(z, 1)] = jnp.sum(gT * gT, axis=0, keepdims=True)[None]
     gN = gT.T
@@ -267,82 +332,95 @@
             return out_ref.at[pl.ds(pl.multiple_of(b * 128, 128), 128)]
         return out_ref.at[pl.ds(pl.multiple_of(b * 128 + half * 64, 64), 64)]
 
-    mine = rows_of(dp)
-    mine[...] = nw.astype(jnp.bfloat16)
+    rows_of(dp)[...] = nw.astype(jnp.bfloat16)
 
     sent = []
 
-    def push(b, half, sem, rsem, to):
-        cp = remote(rows_of(b, half), rows_of(b, half), sem, rsem, to)
+    def push(b, half, rsem, to):
+        cp = remote(rows_of(b, half), rows_of(b, half), ag_s.at[len(sent)], rsem, to)
         cp.start()
         sent.append(cp)
         return cp
 
-    n_sent = [0]
-
-    def nsem():
-        n_sent[0] += 1
-        return ag_s.at[n_sent[0] - 1]
-
-    a1 = {0: push(dp, None, nsem(), a1_r.at[0], wn), 1: push(dp, None, nsem(), a1_r.at[1], wp)}
-    b1, b2, dd, dd2, a2 = {}, {}, {}, {}, {}
-
-    def spread(b, k):
-        b1[0, k] = push(b, None, nsem(), b1_r.at[0, k], un)
-        b1[1, k] = push(b, None, nsem(), b1_r.at[1, k], up)
-
-    def across(b, j):
-        dd[j] = push(b, None, nsem(), dd_r.at[j], sib)
-
-    spread(dp, 0)
-    across(dp, 0)
+    a1, a2, b1, b2, dd = {}, {}, {}, {}, {}
+    for i in range(2):
+        a1[0, i] = push(dp, i, a1_r.at[0, i], wn)
+        a1[1, 1 - i] = push(dp, 1 - i, a1_r.at[1, 1 - i], wp)
+
+    def spread(b, k, h):
+        b1[0, k, h] = push(b, h, b1_r.at[0, k, h], un)
+        b1[1, k, h] = push(b, h, b1_r.at[1, k, h], up)
+
+    def across(b, j, h):
+        dd[j, h] = push(b, h, dd_r.at[j, h], sib)
+
+    def both(b, k):
+        b1[0, k, 0] = push(b, 0, b1_r.at[0, k, 0], un)
+        b1[1, k, 1] = push(b, 1, b1_r.at[1, k, 1], up)
+        b1[0, k, 1] = push(b, 1, b1_r.at[0, k, 1], un)
+        b1[1, k, 0] = push(b, 0, b1_r.at[1, k, 0], up)
+        for h in range(2):
+            across(b, k, h)
+
+    both(dp, 0)
     upd_ref[...] = upd
     nw_ref[...] = nw
-    a1[0].wait_recv()
-    a2[0] = push(wp, 0, nsem(), a2_r.at[0], wn)
-    spread(wp, 1)
-    a1[1].wait_recv()
-    a2[1] = push(wn, 1, nsem(), a2_r.at[1], wp)
-    spread(wn, 2)
-    across(wp, 1)
-    across(wn, 2)
+    a1[0, 0].wait_recv()
+    a2[0] = push(wp, 0, a2_r.at[0], wn)
+    a1[1, 1].wait_recv()
+    a2[1] = push(wn, 1, a2_r.at[1], wp)
+    a1[0, 1].wait_recv()
+    both(wp, 1)
+    a1[1, 0].wait_recv()
+    both(wn, 2)
 
     def onward(k, ww):
-        b1[0, k].wait_recv()
-        b2[0, k] = push(dev(u - 1, ww), 0, nsem(), b2_r.at[0, k], un)
-        across(dev(u - 1, ww), 4 + 2 * k)
-        b1[1, k].wait_recv()
-        b2[1, k] = push(dev(u + 1, ww), 1, nsem(), b2_r.at[1, k], up)
-        across(dev(u + 1, ww), 5 + 2 * k)
+        left, right = dev(u - 1, ww), dev(u + 1, ww)
+        b1[0, k, 0].wait_recv()
+        b2[0, k] = push(left, 0, b2_r.at[0, k], un)
+        b1[1, k, 1].wait_recv()
+        b2[1, k] = push(right, 1, b2_r.at[1, k], up)
+        across(left, 4 + 2 * k, 0)
+        across(right, 5 + 2 * k, 1)
+        b1[0, k, 1].wait_recv()
+        across(left, 4 + 2 * k, 1)
+        b1[1, k, 0].wait_recv()
+        across(right, 5 + 2 * k, 0)
 
     onward(0, w)
-    a2[0].wait_recv()
-    a2[1].wait_recv()
     wf = dev(u, w + 2)
-    spread(wf, 3)
-    across(wf, 3)
+    for h in range(2):
+        a2[h].wait_recv()
+        spread(wf, 3, h)
+        across(wf, 3, h)
     onward(1, w - 1)
     onward(2, w + 1)
     onward(3, w + 2)
     for k, ww in ((0, w), (1, w - 1), (2, w + 1), (3, w + 2)):
-        b2[0, k].wait_recv()
-        b2[1, k].wait_recv()
-        dd2[k] = push(dev(u + 2, ww), None, nsem(), dd2_r.at[k], sib)
-    for j in range(12):
-        dd[j].wait_recv()
-    for k in range(4):
-        dd2[k].wait_recv()
+        for h in range(2):
+            b2[h, k].wait_recv()
+            across(dev(u + 2, ww), 12 + k, h)
+    for cp in dd.values():
+        cp.wait_recv()
 
     for cp in sent:
         cp.wait_send()
-    dq.wait_send()
-    for cp in dx:
-        cp.wait_send()
-    for group in (c1a, c1b, c2a, c2b):
+    for group in (cd, c1a, c1b, c2a, c2b):
         for cp in group.values():
             cp.wait_send()
     for i, (buf, n) in enumerate(((zr, nz), (pr, NPLANE), (ta, NPLANE), (tb, nz))):
         finish(n, buf, ex_s.at[i])
+
+
+def store(a, b, c, d, e, ao, bo, co, do, eo, sem):
+    rows = e.shape[0] // 8
+    pairs = [(e.at[pl.ds(i * rows, rows)], eo.at[pl.ds(i * rows, rows)]) for i in range(8)]
+    pairs += [(a, ao), (b, bo), (c, co), (d, do)]
+    copies = [pltpu.make_async_copy(i, o, sem.at[n]) for n, (i, o) in enumerate(pairs)]
+    for cp in copies:
+        cp.start()
+    for cp in copies:
+        cp.wait()
 
 
 def body(inputs, query_grad, master_weight, row_factor, col_factor, step):
@@ -355,24 +433,30 @@
     DMA = pltpu.SemaphoreType.DMA
     hb = (H + 16, 128)
     vm = pl.BlockSpec(memory_space=pltpu.VMEM)
-    hbm = pl.BlockSpec(memory_space=pl.ANY)
+    hbm = pl.BlockSpec(memory_space=pltpu.HBM)
     outs = pl.pallas_call(
         functools.partial(kernel, nz, T * ndp, rows, W * nz),
         out_shape=[
-            jax.ShapeDtypeStruct((128, W), f32),
-            jax.ShapeDtypeStruct((128, W), f32),
-            jax.ShapeDtypeStruct((1, 128), f32),
-            jax.ShapeDtypeStruct((1, W), f32),
+            pltpu.VMEM((128, W), f32),
+            pltpu.VMEM((128, W), f32),
+            pltpu.VMEM((1, 128), f32),
+            pltpu.VMEM((1, W), f32),
             pltpu.VMEM((rows, W), bf16),
         ],
-        in_specs=[hbm, hbm, vm, vm, vm, pl.BlockSpec(memory_space=pltpu.SMEM)],
+        in_specs=[hbm] * 5 + [pl.BlockSpec(memory_space=pltpu.SMEM)],
         out_specs=[vm, vm, vm, vm, vm],
         scratch_shapes=[
-            pltpu.VMEM((2 * T, W), bf16),
-            pltpu.VMEM((W, 2 * T), bf16),
-            pltpu.VMEM((8, 2 * T, 256), bf16),
+            pltpu.VMEM((128, W), f32),
+            pltpu.VMEM((1, 128), f32),
+            pltpu.VMEM((1, W), f32),
+            DMA((3,)),
+            pltpu.VMEM((T, W), bf16),
+            pltpu.VMEM((W, T), bf16),
+            pltpu.VMEM((16, T, 256), bf16),
             pltpu.VMEM((16, W, 128), f32),
             pltpu.VMEM((4, W, 128), f32),
+            pltpu.VMEM((16, 2) + hb, i16),
+            pltpu.VMEM((16, 2) + hb, i16),
             pltpu.VMEM((2, 4) + hb, i16),
             pltpu.VMEM((2, 4) + hb, i16),
             pltpu.VMEM((2, 4, 2) + hb, i16),
@@ -385,20 +469,31 @@
             pltpu.VMEM((NPLANE, 1, W), f32),
             pltpu.VMEM((NPLANE, 1, 128), f32),
             pltpu.VMEM((nz, 1, 128), f32),
-            DMA((16,)), DMA, DMA((17,)), DMA((17,)),
+            DMA((32,)), DMA, DMA((16,)), DMA((16,)),
             DMA((2, 4)), DMA((2, 4)), DMA((2, 4, 2)), DMA((2, 4, 2)),
             DMA((2,)), DMA((2,)), DMA((2, 2)), DMA((2, 2)),
             DMA((4,)), DMA, DMA, DMA, DMA,
             pltpu.SemaphoreType.REGULAR, pltpu.SemaphoreType.REGULAR,
-            DMA((40,)), DMA((2,)), DMA((2,)), DMA((2, 4)), DMA((2, 4)), DMA((12,)), DMA((4,)),
+            DMA((64,)), DMA((2, 2)), DMA((2,)), DMA((2, 4, 2)), DMA((2, 4)), DMA((16, 2)),
         ],
         compiler_params=pltpu.CompilerParams(
             collective_id=0, has_side_effects=True, vmem_limit_bytes=44 * 2**20
         ),
-    )(
-        inputs, query_grad, master_weight,
-        row_factor.reshape(1, 128), col_factor.reshape(1, W), step,
-    )
+    )(*[
+        pltpu.with_memory_space_constraint(a, pltpu.HBM)
+        for a in (
+            inputs, query_grad, master_weight,
+            row_factor.reshape(1, 128), col_factor.reshape(1, W),
+        )
+    ], step)
+    outs = pl.pallas_call(
+        store,
+        out_shape=[jax.ShapeDtypeStruct(o.shape, o.dtype) for o in outs],
+        in_specs=[vm] * 5,
+        out_specs=[hbm] * 5,
+        scratch_shapes=[DMA((12,))],
+        compiler_params=pltpu.CompilerParams(vmem_limit_bytes=8 * 2**20),
+    )(*outs)
     return outs[0], outs[1], outs[2].reshape(128), outs[3].reshape(W), outs[4]
 
 

time: 77.4 us -> 68.5 us (0.89)
  local copies, waits for them, and re-layouts: 7.92 us -> 0 us
  Pallas kernels: 68 us -> 67.1 us
    unnamed x13 -> x0, local copies, waits for them, and re-layouts: 7.92 us -> none
    pallas_call x1, Pallas kernels: 68 us -> 64.8 us  [body(): pl.pallas_call(functools.partial(kernel, nz, T * ndp, rows, W * nz), out_...]
    pallas_call x0 -> x1, Pallas kernels: none -> 2.27 us  [body(): pl.pallas_call(store, out_shape=[jax.ShapeDtypeStruct(o.shape, o.dtype) f...]
where the time goes in v2:
time: 68.5 us; the launch traced here: 68.4 us
  Pallas kernels  67.1 us (98%)
  between operations  1.29 us (2%)
    pallas_call x1, Pallas kernels, body(): pl.pallas_call(functools.partial(kernel, nz, T * ndp, rows, W * nz), out_...  64.8 us
    pallas_call x1, Pallas kernels, body(): pl.pallas_call(store, out_shape=[jax.ShapeDtypeStruct(o.shape, o.dtype) f...  2.27 us

profile of v2, /device:TPU:1, one launch (start us, length us, event | category | flops | bytes accessed | tf_op | source)
XLA Modules:
  0.0 68.4 jit_solution(6132758332313742508)
XLA Ops:
  1.3 64.8 %shard_map.101 = (f32[128,512]{1,0:T(8,128)S(1)}, f32[128,512]{1,0:T(8,128)S(1)}, f32[1,128]{1,0:T(1,128)S(1)}, f32[1,512]{1,0:T(1,128)S(1)}, bf16[4096,512]{1,0:T(8,128)(2,1)S(1)}) custom-call(bf16[768,4096]{1,0:T(8,128)(2,1)} %x_hbm.1, bf16[768,512]{1,0:T(8,128)(2,1)} %q_hbm.1, f32[128,512]{1,0:T(8,128)} %mw_hbm.1, f32[1,128]{1,0:T(1,128)} %bitcast.5, ...), custom_call_target="tpu_custom_call" | custom-call | tf_op jit(solution)/shard_map/pallas_call | solution.py:437
  66.1 2.3 %shard_map.102 = (f32[128,512]{1,0:T(8,128)}, f32[128,512]{1,0:T(8,128)}, f32[1,128]{1,0:T(1,128)}, f32[1,512]{1,0:T(1,128)}, bf16[4096,512]{1,0:T(8,128)(2,1)}) custom-call(f32[128,512]{1,0:T(8,128)S(1)} %get-tuple-element.15.a, f32[128,512]{1,0:T(8,128)S(1)} %get-tuple-element.16.b, f32[1,128]{1,0:T(1,128)S(1)} %get-tuple-element.17.c, ...), custom_call_target="tpu_custom_call" | custom-call | tf_op jit(solution)/shard_map/pallas_call | solution.py:489

commit v3 on v2

--- a/solution.py
+++ b/solution.py
@@ -48,25 +48,29 @@
     H = W // 2
     dp = lax.axis_index("dp")
     z = lax.axis_index("mp")
-    c = dp % 2
-    cx = dp // (NY * NC)
-    cy = (dp // NC) % NY
+    c = lax.rem(dp, NC)
+    cx = lax.div(dp, NY * NC)
+    cy = lax.rem(lax.div(dp, NC), NY)
     sib = dp + 1 - 2 * c
     cs = 1 - c
     u = cx * (1 - c) + cy * c
     w = cy * (1 - c) + cx * c
     su = NY * NC - (NY * NC - NC) * c
     sw = NC + (NY * NC - NC) * c
-    us, ws, sus, sws = w, u, sw, su
-
-    def dev(uu, ww):
-        return ((uu + 8) % 4) * su + ((ww + 8) % 4) * sw + c
-
-    def sdev(uu, ww):
-        return ((uu + 8) % 4) * sus + ((ww + 8) % 4) * sws + cs
-
-    un, up = dev(u + 1, w), dev(u - 1, w)
-    wn, wp = dev(u, w + 1), dev(u, w - 1)
+    ru = [lax.rem(u + i, 4) * su for i in range(4)]
+    rw = [lax.rem(w + i, 4) * sw for i in range(4)]
+    rx = [lax.rem(cx + i, NX) * (NY * NC) for i in range(NX)]
+    ry = [lax.rem(cy + i, NY) * NC for i in range(NY)]
+    rz = [lax.rem(z + i, nz) for i in range(nz)]
+
+    def dev(i, j):
+        return ru[i % 4] + rw[j % 4] + c
+
+    def sdev(i, j):
+        return rw[i % 4] + ru[j % 4] + cs
+
+    un, up = dev(1, 0), dev(-1, 0)
+    wn, wp = dev(0, 1), dev(0, -1)
 
     def cols_of(b):
         return pl.ds(pl.multiple_of(b * 128, 128), 128)
@@ -83,7 +87,7 @@
     def load(side, p):
         for s in (2 * p, 2 * p + 1):
             o = (FAR[s // 4], FAR[s % 4])
-            b = dev(u + o[0], w + o[1]) if side else sdev(us + o[0], ws + o[1])
+            b = dev(*o) if side else sdev(*o)
             j = 16 * side + s
             cp = pltpu.make_async_copy(
                 x_hbm.at[:, cols_of(b)],
@@ -97,7 +101,7 @@
         load(side, p)
 
     bar = pltpu.get_barrier_semaphore()
-    zn, zp = (z + 1) % nz, (z + nz - 1) % nz
+    zn, zp = rz[1 % nz], rz[nz - 1]
     for d in (sib, un, up, wn, wp):
         pl.semaphore_signal(bar, 1, device_id=(d, z), device_id_type=MESH)
     for zz in (zn, zp):
@@ -169,7 +173,7 @@
             cp.start()
             c1a[d, k] = cp
     pl.semaphore_wait(zs1, 2)
-    for zz in ((z + 2) % nz, (z + nz - 2) % nz):
+    for zz in (rz[2 % nz], rz[nz - 2]):
         pl.semaphore_signal(zs2, 1, device_id=(dp, zz), device_id_type=MESH)
 
     c1b = {}
@@ -200,6 +204,45 @@
             )
         for d in range(2):
             send1b(d, k, d)
+
+    c2a, c2b = {}, {}
+
+    def send2b(d, h):
+        to = wn if d == 0 else wp
+        cp = remote(s2b.at[d, h], r2b.at[d, h], s2b_s.at[d, h], s2b_r.at[d, h], to)
+        cp.start()
+        c2b[d, h] = cp
+
+    def gathered(k, h):
+        c1b[0, k, h].wait_recv()
+        c1b[1, k, h].wait_recv()
+        R[k, h * H : h * H + H, :] = (
+            S[12 + k, h * H : h * H + H, :]
+            + decode(r1b.at[0, k, h], H)
+            + decode(r1b.at[1, k, h], H)
+        )
+
+    def second(k):
+        if k == 0:
+            gathered(k, 0)
+            gathered(k, 1)
+            for d, to in ((0, wn), (1, wp)):
+                encode(R[0, d * H : d * H + H, :], s2a.at[d])
+                cp = remote(s2a.at[d], r2a.at[d], s2a_s.at[d], s2a_r.at[d], to)
+                cp.start()
+                c2a[d] = cp
+        else:
+            d = k - 1
+            gathered(k, 1 - d)
+            encode(R[k, (1 - d) * H : (1 - d) * H + H, :], s2b.at[d, 1 - d])
+            send2b(d, 1 - d)
+            gathered(k, d)
+
+    def second_far(k):
+        d = k - 1
+        c2a[d].wait_recv()
+        encode(R[k, d * H : d * H + H, :] + decode(r2a.at[d], H), s2b.at[d, d])
+        send2b(d, d)
 
     theirs(4)
     give(4)
@@ -214,53 +257,25 @@
     mine(5)
     with_far(0)
     at_once(2)
+    at_once(3)
     with_far(1)
-    theirs(6)
-    give(6)
-    at_once(3)
+    for p in (6, 7):
+        theirs(p)
+        give(p)
     with_far(2)
-    theirs(7)
-    give(7)
     mine(6)
+    mine(7)
     with_far(3)
-    mine(7)
     for s in range(12, 16):
         total(s)
-
     pl.semaphore_wait(zs2, 2)
-
-    c2a, c2b = {}, {}
-
-    def send2b(d, h):
-        to = wn if d == 0 else wp
-        cp = remote(s2b.at[d, h], r2b.at[d, h], s2b_s.at[d, h], s2b_r.at[d, h], to)
-        cp.start()
-        c2b[d, h] = cp
-
-    for k in range(4):
-        for h in range(2):
-            c1b[0, k, h].wait_recv()
-            c1b[1, k, h].wait_recv()
-            R[k, h * H : h * H + H, :] = (
-                S[12 + k, h * H : h * H + H, :]
-                + decode(r1b.at[0, k, h], H)
-                + decode(r1b.at[1, k, h], H)
-            )
-        if k == 0:
-            for d, to in ((0, wn), (1, wp)):
-                encode(R[0, d * H : d * H + H, :], s2a.at[d])
-                cp = remote(s2a.at[d], r2a.at[d], s2a_s.at[d], s2a_r.at[d], to)
-                cp.start()
-                c2a[d] = cp
-        elif k < 3:
-            d = k - 1
-            h = 1 - d
-            encode(R[k, h * H : h * H + H, :], s2b.at[d, h])
-            send2b(d, h)
-            c2a[d].wait_recv()
-            h = d
-            encode(R[k, h * H : h * H + H, :] + decode(r2a.at[d], H), s2b.at[d, h])
-            send2b(d, h)
+    second(0)
+    second(1)
+    second(2)
+    second_far(1)
+    second_far(2)
+    gathered(3, 0)
+    gathered(3, 1)
     for h in range(2):
         c2b[0, h].wait_recv()
         c2b[1, h].wait_recv()
@@ -275,28 +290,28 @@
     gN = gT.T
     pr[pl.ds(dp, 1)] = jnp.sum(gN * gN, axis=0, keepdims=True)[None]
 
-    def to_plane(i, buf, ssem, rsem):
-        peer = (dp + i) % NPLANE
-        return remote(buf.at[pl.ds(dp, 1)], buf.at[pl.ds(dp, 1)], ssem, rsem, peer)
-
-    def to_z(i, buf, ssem, rsem):
-        peer = (z + i) % nz
-        return remote(buf.at[pl.ds(z, 1)], buf.at[pl.ds(z, 1)], ssem, rsem, dp, peer)
-
-    def exchange(n, to, buf, ssem, rsem):
-        def body(i, carry):
-            to(i, buf, ssem, rsem).start()
-            return carry
-
-        lax.fori_loop(1, n, body, 0)
+    far_plane = sorted(
+        ((i, j, k) for i in range(NX) for j in range(NY) for k in range(NC) if i or j or k),
+        key=lambda o: -(min(o[0], NX - o[0]) + min(o[1], NY - o[1])),
+    )
+    far_z = sorted(range(1, nz), key=lambda i: -min(i, nz - i))
+
+    def to_plane(buf, ssem, rsem):
+        for i, j, k in far_plane:
+            peer = rx[i] + ry[j] + (cs if k else c)
+            remote(buf.at[pl.ds(dp, 1)], buf.at[pl.ds(dp, 1)], ssem, rsem, peer).start()
+
+    def to_z(buf, ssem, rsem):
+        for i in far_z:
+            remote(buf.at[pl.ds(z, 1)], buf.at[pl.ds(z, 1)], ssem, rsem, dp, rz[i]).start()
 
     def finish(n, buf, rsem):
         part = buf.at[pl.ds(0, n - 1)]
         cp = pltpu.make_async_copy(part, part, rsem)
         cp.wait()
 
-    exchange(nz, to_z, zr, ex_s.at[0], zr_r)
-    exchange(NPLANE, to_plane, pr, ex_s.at[1], pr_r)
+    to_z(zr, ex_s.at[0], zr_r)
+    to_plane(pr, ex_s.at[1], pr_r)
     mw = mw_ref[...]
     wsum = jnp.sum(mw * mw)
     stepv = jnp.full((1, 128), step_ref[0].astype(jnp.float32), jnp.float32)
@@ -316,10 +331,13 @@
 
     lane = lax.broadcasted_iota(jnp.int32, (1, 1, 128), 2)
     ta[pl.ds(dp, 1)] = jnp.where(lane < 64, rsum, wsum)
-    exchange(NPLANE, to_plane, ta, ex_s.at[2], ta_r)
+    to_plane(ta, ex_s.at[2], ta_r)
+    for group in (cd, c1a, c1b, c2a, c2b):
+        for cp in group.values():
+            cp.wait_send()
     finish(NPLANE, ta, ta_r)
     tb[pl.ds(z, 1)] = jnp.sum(ta[...], axis=0, keepdims=True)
-    exchange(nz, to_z, tb, ex_s.at[3], tb_r)
+    to_z(tb, ex_s.at[3], tb_r)
     finish(nz, tb, tb_r)
     tot = jnp.sum(tb[...], axis=0) / (total_rows * total_cols)
     clip = jnp.maximum(1.0, jnp.sqrt(tot[:, 0:1]))
@@ -362,20 +380,20 @@
         for h in range(2):
             across(b, k, h)
 
+    for h in range(2):
+        a2[h] = push(dp, h, a2_r.at[h], dev(0, 2))
     both(dp, 0)
     upd_ref[...] = upd
     nw_ref[...] = nw
     a1[0, 0].wait_recv()
-    a2[0] = push(wp, 0, a2_r.at[0], wn)
-    a1[1, 1].wait_recv()
-    a2[1] = push(wn, 1, a2_r.at[1], wp)
     a1[0, 1].wait_recv()
     both(wp, 1)
+    a1[1, 1].wait_recv()
     a1[1, 0].wait_recv()
     both(wn, 2)
 
     def onward(k, ww):
-        left, right = dev(u - 1, ww), dev(u + 1, ww)
+        left, right = dev(-1, ww), dev(1, ww)
         b1[0, k, 0].wait_recv()
         b2[0, k] = push(left, 0, b2_r.at[0, k], un)
         b1[1, k, 1].wait_recv()
@@ -387,27 +405,24 @@
         b1[1, k, 0].wait_recv()
         across(right, 5 + 2 * k, 0)
 
-    onward(0, w)
-    wf = dev(u, w + 2)
+    wf = dev(0, 2)
     for h in range(2):
         a2[h].wait_recv()
         spread(wf, 3, h)
         across(wf, 3, h)
-    onward(1, w - 1)
-    onward(2, w + 1)
-    onward(3, w + 2)
-    for k, ww in ((0, w), (1, w - 1), (2, w + 1), (3, w + 2)):
+    onward(0, 0)
+    onward(1, -1)
+    onward(2, 1)
+    onward(3, 2)
+    for k, ww in ((0, 0), (1, -1), (2, 1), (3, 2)):
         for h in range(2):
             b2[h, k].wait_recv()
-            across(dev(u + 2, ww), 12 + k, h)
+            across(dev(2, ww), 12 + k, h)
     for cp in dd.values():
         cp.wait_recv()
 
     for cp in sent:
         cp.wait_send()
-    for group in (cd, c1a, c1b, c2a, c2b):
-        for cp in group.values():
-            cp.wait_send()
     for i, (buf, n) in enumerate(((zr, nz), (pr, NPLANE), (ta, NPLANE), (tb, nz))):
         finish(n, buf, ex_s.at[i])
 

time: 68.5 us -> 67 us (0.978)
  Pallas kernels: 67.1 us -> 65.6 us
    pallas_call x1, Pallas kernels: 64.8 us -> 63.3 us  [body(): pl.pallas_call(functools.partial(kernel, nz, T * ndp, rows, W * nz), out_...]
where the time goes in v3:
time: 67 us; the launch traced here: 66.9 us
  Pallas kernels  65.6 us (98%)
  between operations  1.29 us (2%)
    pallas_call x1, Pallas kernels, body(): pl.pallas_call(functools.partial(kernel, nz, T * ndp, rows, W * nz), out_...  63.3 us
    pallas_call x1, Pallas kernels, body(): pl.pallas_call(store, out_shape=[jax.ShapeDtypeStruct(o.shape, o.dtype) f...  2.27 us

profile of v3, /device:TPU:1, one launch (start us, length us, event | category | flops | bytes accessed | tf_op | source)
XLA Modules:
  0.0 66.9 jit_solution(3324257901241044769)
XLA Ops:
  1.3 63.3 %shard_map.101 = (f32[128,512]{1,0:T(8,128)S(1)}, f32[128,512]{1,0:T(8,128)S(1)}, f32[1,128]{1,0:T(1,128)S(1)}, f32[1,512]{1,0:T(1,128)S(1)}, bf16[4096,512]{1,0:T(8,128)(2,1)S(1)}) custom-call(bf16[768,4096]{1,0:T(8,128)(2,1)} %x_hbm.1, bf16[768,512]{1,0:T(8,128)(2,1)} %q_hbm.1, f32[128,512]{1,0:T(8,128)} %mw_hbm.1, f32[1,128]{1,0:T(1,128)} %bitcast.5, ...), custom_call_target="tpu_custom_call" | custom-call | tf_op jit(solution)/shard_map/pallas_call | solution.py:452
  64.6 2.3 %shard_map.102 = (f32[128,512]{1,0:T(8,128)}, f32[128,512]{1,0:T(8,128)}, f32[1,128]{1,0:T(1,128)}, f32[1,512]{1,0:T(1,128)}, bf16[4096,512]{1,0:T(8,128)(2,1)}) custom-call(f32[128,512]{1,0:T(8,128)S(1)} %get-tuple-element.15.a, f32[128,512]{1,0:T(8,128)S(1)} %get-tuple-element.16.b, f32[1,128]{1,0:T(1,128)S(1)} %get-tuple-element.17.c, ...), custom_call_target="tpu_custom_call" | custom-call | tf_op jit(solution)/shard_map/pallas_call | solution.py:504

commit v4 on v3

--- a/solution.py
+++ b/solution.py
@@ -115,39 +115,40 @@
     cq.wait()
     qT[...] = qcat[...].T
 
-    def matmul(side, p):
-        j = 8 * side + p
-        loads[2 * j].wait()
-        loads[2 * j + 1].wait()
-        return jnp.dot(qT[...], X[j], preferred_element_type=jnp.float32)
-
-    def theirs(p):
-        acc = matmul(0, p)
-        for i in range(2):
+    cd = {}
+
+    def work(theirs, mine):
+        jobs = [8 * 0 + p for p in theirs] + [8 + p for p in mine]
+        for j in jobs:
+            loads[2 * j].wait()
+            loads[2 * j + 1].wait()
+        for j in jobs:
+            acc = jnp.dot(qT[...], X[j], preferred_element_type=jnp.float32)
+            for i in range(2):
+                part = acc[:, 128 * i : 128 * i + 128]
+                if j >= 8:
+                    S[2 * (j - 8) + i] = part
+                else:
+                    for h in range(2):
+                        encode(part[h * H : h * H + H], sd.at[2 * j + i, h])
+
+    def give(*pairs):
+        for p in pairs:
+            for s in (2 * p, 2 * p + 1):
+                cd[s] = remote(sd.at[s], rd.at[s], d_send.at[s], d_recv.at[s], sib)
+                cd[s].start()
+
+    def total(*blocks):
+        for s in blocks:
+            cd[s].wait_recv()
+        for s in blocks:
             for h in range(2):
-                encode(acc[h * H : h * H + H, 128 * i : 128 * i + 128], sd.at[2 * p + i, h])
-
-    cd = {}
-
-    def give(p):
-        for s in (2 * p, 2 * p + 1):
-            cd[s] = remote(sd.at[s], rd.at[s], d_send.at[s], d_recv.at[s], sib)
-            cd[s].start()
-
-    def mine(p):
-        acc = matmul(1, p)
-        S[2 * p] = acc[:, 0:128]
-        S[2 * p + 1] = acc[:, 128:256]
-
-    def total(s):
-        cd[s].wait_recv()
-        for h in range(2):
-            S[s, h * H : h * H + H, :] = S[s, h * H : h * H + H, :] + decode(rd.at[s, h], H)
-
-    theirs(0)
+                S[s, h * H : h * H + H, :] = S[s, h * H : h * H + H, :] + decode(rd.at[s, h], H)
+
+    work((0,), ())
     pl.semaphore_wait(bar, 7)
     give(0)
-    theirs(1)
+    work((1,), (0, 1))
     give(1)
     params = [
         pltpu.make_async_copy(a, b, p_sem.at[i])
@@ -158,20 +159,25 @@
 
     for zz in (zn, zp):
         pl.semaphore_signal(zs1, 1, device_id=(dp, zz), device_id_type=MESH)
-    mine(0)
-    mine(1)
-    theirs(2)
-    give(2)
-
     c1a = {}
-    for k in range(4):
-        total(k)
-        for d in range(2):
-            encode(S[k, d * H : d * H + H, :], s1a.at[d, k])
-        for d, to in ((0, un), (1, up)):
-            cp = remote(s1a.at[d, k], r1a.at[d, k], s1a_s.at[d, k], s1a_r.at[d, k], to)
-            cp.start()
-            c1a[d, k] = cp
+
+    def first(*ks):
+        total(*ks)
+        for k in ks:
+            for d in range(2):
+                encode(S[k, d * H : d * H + H, :], s1a.at[d, k])
+        for k in ks:
+            for d, to in ((0, un), (1, up)):
+                cp = remote(s1a.at[d, k], r1a.at[d, k], s1a_s.at[d, k], s1a_r.at[d, k], to)
+                cp.start()
+                c1a[d, k] = cp
+
+    first(0)
+    first(1)
+    work((2, 4), (2, 4))
+    give(2, 4)
+    first(2)
+    first(3)
     pl.semaphore_wait(zs1, 2)
     for zz in (rz[2 % nz], rz[nz - 2]):
         pl.semaphore_signal(zs2, 1, device_id=(dp, zz), device_id_type=MESH)
@@ -186,24 +192,29 @@
         cp.start()
         c1b[d, k, h] = cp
 
-    def at_once(k):
-        for d in range(2):
-            h = 1 - d
-            total(4 * (1 + d) + k)
-            encode(S[4 * (1 + d) + k, h * H : h * H + H, :], s1b.at[d, k, h])
-        for d in range(2):
-            send1b(d, k, 1 - d)
-
-    def with_far(k):
-        for d in range(2):
-            h = d
-            c1a[d, k].wait_recv()
-            encode(
-                S[4 * (1 + d) + k, h * H : h * H + H, :] + decode(r1a.at[d, k], H),
-                s1b.at[d, k, h],
-            )
-        for d in range(2):
-            send1b(d, k, d)
+    def at_once(*ks):
+        total(*(4 * g + k for k in ks for g in (1, 2)))
+        for k in ks:
+            for d in range(2):
+                h = 1 - d
+                encode(S[4 * (1 + d) + k, h * H : h * H + H, :], s1b.at[d, k, h])
+        for k in ks:
+            for d in range(2):
+                send1b(d, k, 1 - d)
+
+    def with_far(*ks):
+        for k in ks:
+            for d in range(2):
+                c1a[d, k].wait_recv()
+        for k in ks:
+            for d in range(2):
+                encode(
+                    S[4 * (1 + d) + k, d * H : d * H + H, :] + decode(r1a.at[d, k], H),
+                    s1b.at[d, k, d],
+                )
+        for k in ks:
+            for d in range(2):
+                send1b(d, k, d)
 
     c2a, c2b = {}, {}
 
@@ -213,21 +224,23 @@
         cp.start()
         c2b[d, h] = cp
 
-    def gathered(k, h):
-        c1b[0, k, h].wait_recv()
-        c1b[1, k, h].wait_recv()
-        R[k, h * H : h * H + H, :] = (
-            S[12 + k, h * H : h * H + H, :]
-            + decode(r1b.at[0, k, h], H)
-            + decode(r1b.at[1, k, h], H)
-        )
+    def gathered(k, *hs):
+        for h in hs:
+            c1b[0, k, h].wait_recv()
+            c1b[1, k, h].wait_recv()
+        for h in hs:
+            R[k, h * H : h * H + H, :] = (
+                S[12 + k, h * H : h * H + H, :]
+                + decode(r1b.at[0, k, h], H)
+                + decode(r1b.at[1, k, h], H)
+            )
 
     def second(k):
         if k == 0:
-            gathered(k, 0)
-            gathered(k, 1)
+            gathered(k, 0, 1)
+            for d in range(2):
+                encode(R[0, d * H : d * H + H, :], s2a.at[d])
             for d, to in ((0, wn), (1, wp)):
-                encode(R[0, d * H : d * H + H, :], s2a.at[d])
                 cp = remote(s2a.at[d], r2a.at[d], s2a_s.at[d], s2a_r.at[d], to)
                 cp.start()
                 c2a[d] = cp
@@ -244,41 +257,30 @@
         encode(R[k, d * H : d * H + H, :] + decode(r2a.at[d], H), s2b.at[d, d])
         send2b(d, d)
 
-    theirs(4)
-    give(4)
-    mine(2)
-    mine(4)
     at_once(0)
+    with_far(0)
     at_once(1)
-    for p in (3, 5):
-        theirs(p)
-        give(p)
-    mine(3)
-    mine(5)
-    with_far(0)
+    work((3, 5), (3, 5))
+    give(3, 5)
+    with_far(1)
     at_once(2)
+    work((6, 7), (6, 7))
+    give(6, 7)
+    with_far(2)
     at_once(3)
-    with_far(1)
-    for p in (6, 7):
-        theirs(p)
-        give(p)
-    with_far(2)
-    mine(6)
-    mine(7)
     with_far(3)
-    for s in range(12, 16):
-        total(s)
+    total(12, 13, 14, 15)
     pl.semaphore_wait(zs2, 2)
     second(0)
     second(1)
     second(2)
     second_far(1)
     second_far(2)
-    gathered(3, 0)
-    gathered(3, 1)
+    gathered(3, 0, 1)
     for h in range(2):
         c2b[0, h].wait_recv()
         c2b[1, h].wait_recv()
+    for h in range(2):
         R[3, h * H : h * H + H, :] = (
             R[3, h * H : h * H + H, :] + decode(r2b.at[0, h], H) + decode(r2b.at[1, h], H)
         )

time: 67 us -> 66.1 us (0.987)
  Pallas kernels: 65.6 us -> 64.7 us
    pallas_call x1, Pallas kernels: 63.3 us -> 62.4 us  [body(): pl.pallas_call(functools.partial(kernel, nz, T * ndp, rows, W * nz), out_...]
where the time goes in v4:
time: 66.1 us; the launch traced here: 66 us
  Pallas kernels  64.7 us (98%)
  between operations  1.29 us (2%)
    pallas_call x1, Pallas kernels, body(): pl.pallas_call(functools.partial(kernel, nz, T * ndp, rows, W * nz), out_...  62.4 us
    pallas_call x1, Pallas kernels, body(): pl.pallas_call(store, out_shape=[jax.ShapeDtypeStruct(o.shape, o.dtype) f...  2.27 us

profile of v4, /device:TPU:1, one launch (start us, length us, event | category | flops | bytes accessed | tf_op | source)
XLA Modules:
  0.0 66.0 jit_solution(6763393509071771734)
XLA Ops:
  1.3 62.4 %shard_map.101 = (f32[128,512]{1,0:T(8,128)S(1)}, f32[128,512]{1,0:T(8,128)S(1)}, f32[1,128]{1,0:T(1,128)S(1)}, f32[1,512]{1,0:T(1,128)S(1)}, bf16[4096,512]{1,0:T(8,128)(2,1)S(1)}) custom-call(bf16[768,4096]{1,0:T(8,128)(2,1)} %x_hbm.1, bf16[768,512]{1,0:T(8,128)(2,1)} %q_hbm.1, f32[128,512]{1,0:T(8,128)} %mw_hbm.1, f32[1,128]{1,0:T(1,128)} %bitcast.5, ...), custom_call_target="tpu_custom_call" | custom-call | tf_op jit(solution)/shard_map/pallas_call | solution.py:454
  63.7 2.3 %shard_map.102 = (f32[128,512]{1,0:T(8,128)}, f32[128,512]{1,0:T(8,128)}, f32[1,128]{1,0:T(1,128)}, f32[1,512]{1,0:T(1,128)}, bf16[4096,512]{1,0:T(8,128)(2,1)}) custom-call(f32[128,512]{1,0:T(8,128)S(1)} %get-tuple-element.15.a, f32[128,512]{1,0:T(8,128)S(1)} %get-tuple-element.16.b, f32[1,128]{1,0:T(1,128)S(1)} %get-tuple-element.17.c, ...), custom_call_target="tpu_custom_call" | custom-call | tf_op jit(solution)/shard_map/pallas_call | solution.py:506

commit v5 on v4

--- a/solution.py
+++ b/solution.py
@@ -263,15 +263,16 @@
     work((3, 5), (3, 5))
     give(3, 5)
     with_far(1)
-    at_once(2)
     work((6, 7), (6, 7))
     give(6, 7)
+    at_once(2)
     with_far(2)
+    total(12)
+    second(0)
     at_once(3)
     with_far(3)
-    total(12, 13, 14, 15)
+    total(13, 14, 15)
     pl.semaphore_wait(zs2, 2)
-    second(0)
     second(1)
     second(2)
     second_far(1)

time: 66.1 us -> 65.3 us (0.988)
  Pallas kernels: 64.7 us -> 63.9 us
    pallas_call x1, Pallas kernels: 62.4 us -> 61.7 us  [body(): pl.pallas_call(functools.partial(kernel, nz, T * ndp, rows, W * nz), out_...]
where the time goes in v5:
time: 65.3 us; the launch traced here: 65.2 us
  Pallas kernels  63.9 us (98%)
  between operations  1.29 us (2%)
    pallas_call x1, Pallas kernels, body(): pl.pallas_call(functools.partial(kernel, nz, T * ndp, rows, W * nz), out_...  61.7 us
    pallas_call x1, Pallas kernels, body(): pl.pallas_call(store, out_shape=[jax.ShapeDtypeStruct(o.shape, o.dtype) f...  2.27 us

profile of v5, /device:TPU:1, one launch (start us, length us, event | category | flops | bytes accessed | tf_op | source)
XLA Modules:
  0.0 65.2 jit_solution(8979580235902254742)
XLA Ops:
  1.3 61.7 %shard_map.101 = (f32[128,512]{1,0:T(8,128)S(1)}, f32[128,512]{1,0:T(8,128)S(1)}, f32[1,128]{1,0:T(1,128)S(1)}, f32[1,512]{1,0:T(1,128)S(1)}, bf16[4096,512]{1,0:T(8,128)(2,1)S(1)}) custom-call(bf16[768,4096]{1,0:T(8,128)(2,1)} %x_hbm.1, bf16[768,512]{1,0:T(8,128)(2,1)} %q_hbm.1, f32[128,512]{1,0:T(8,128)} %mw_hbm.1, f32[1,128]{1,0:T(1,128)} %bitcast.5, ...), custom_call_target="tpu_custom_call" | custom-call | tf_op jit(solution)/shard_map/pallas_call | solution.py:455
  63.0 2.3 %shard_map.102 = (f32[128,512]{1,0:T(8,128)}, f32[128,512]{1,0:T(8,128)}, f32[1,128]{1,0:T(1,128)}, f32[1,512]{1,0:T(1,128)}, bf16[4096,512]{1,0:T(8,128)(2,1)}) custom-call(f32[128,512]{1,0:T(8,128)S(1)} %get-tuple-element.15.a, f32[128,512]{1,0:T(8,128)S(1)} %get-tuple-element.16.b, f32[1,128]{1,0:T(1,128)S(1)} %get-tuple-element.17.c, ...), custom_call_target="tpu_custom_call" | custom-call | tf_op jit(solution)/shard_map/pallas_call | solution.py:507
